TPU v7x, 32 devices: a whole 2x2x4 slice. The times are simulated.
32 devices in a mesh: grp: 2 (over x), mk: 8 (over z, y), tile: 2 (over core).
Axes of the slice: x: 2, y: 2, z: 4, core: 2. Of those that a mesh axis runs over, the one named last changes fastest.
Arguments:
- dosage: bfloat16 [3072, 16384], P(('grp', 'tile'), 'mk'), parts along dimension 0, may hold values from 0 to 2
- allele_freq: float32 [32768], P(('grp', 'mk')), parts along dimension 0, may hold values from 0.05 to 0.5
- present: int32 [256, 3072], P('mk', ('grp', 'tile')), parts along dimension 1, may hold values 0 or 1
- panel_rows: int32 [32], P('grp'), parts along dimension 0, may hold values from 1 to 192, 1536 in all
Outputs:
- panels: float32 [6144, 1536], P(('grp', 'mk', 'tile')), parts along dimension 0
There are 2 independent parts, one for each index of `grp`. A program takes and returns all parts, laid end to end along the dimension named above; each array names one. Nothing has to cross between parts.
Inputs may be any that keep to these rules, and one draw needn't show every extreme that they name: `panel_rows`: the counts sum to 1536.
All inputs are finite; a program needn't handle non-finite values. No bound on the sum of `present` on one device may be relied on, other than what follows from the above.
Results may differ from a plain program's by a relative error of at most 0.0011.
Values may be sent and summed in bfloat16 or wider, within the bound.
A program may use at most 64 MiB of HBM per device.

v0:
```python
import jax
import jax.numpy as jnp
from jax import lax
from jax.sharding import PartitionSpec as P


def local(dosage, allele_freq, present, panel_rows):
    tile_count = lax.axis_size("tile")
    local_markers = dosage.shape[1]
    marker_total = local_markers * lax.axis_size("mk")
    flags = jnp.repeat(present.T, local_markers // present.shape[0], axis=1).astype(jnp.float32)
    twice_freq = 2.0 * allele_freq
    scaled = (dosage.astype(jnp.float32) - twice_freq) / jnp.sqrt(twice_freq * (1.0 - allele_freq))
    standard = (flags * scaled).astype(jnp.bfloat16)
    all_rows = lax.all_gather(standard, "tile", axis=0, tiled=True)
    samples = all_rows.shape[0]
    owner_count = lax.axis_size("mk") * tile_count
    panel_max = 2 * samples // owner_count
    starts = jnp.cumsum(panel_rows) - panel_rows
    row_ids = jnp.arange(panel_max * tile_count * lax.axis_size("mk"), dtype=jnp.int32)
    owner_ids = row_ids // panel_max
    within = row_ids - owner_ids * panel_max
    sample_ids = jnp.take(starts, owner_ids) + within
    live = within < jnp.take(panel_rows, owner_ids)
    picked = jnp.take(all_rows, jnp.clip(sample_ids, 0, samples - 1), axis=0)
    picked = jnp.where(live[:, None], picked, jnp.zeros((), jnp.bfloat16))
    product = jnp.einsum("rm,sm->rs", picked, standard, preferred_element_type=jnp.float32)
    pair_rows = lax.psum_scatter(
        product * (1.0 / marker_total), "mk", scatter_dimension=0, tiled=True
    )
    return lax.all_to_all(pair_rows, "tile", split_axis=0, concat_axis=1, tiled=True)


def solution(mesh):
    in_specs = (P(("grp", "tile"), "mk"), P(("grp", "mk")), P("mk", ("grp", "tile")), P("grp"))
    out_specs = P(("grp", "mk", "tile"), None)
    return jax.shard_map(local, mesh=mesh, in_specs=in_specs, out_specs=out_specs, check_vma=False)
```

profile of v0, /device:TPU:0, one launch (start us, length us, event | category | flops | bytes accessed | tf_op | source)
XLA Modules:
  0.0 279.3 jit_solution(269421417285457136)
XLA Ops:
  6.5 0.0 all-gather.2.cloned.1.call-start
  6.5 0.7 broadcast_multiply_fusion
  7.2 0.9 convert_bitcast_fusion
  8.1 3.1 %broadcast_in_dim.38 = f32[768,32,64]{0,2,1:T(8,128)} broadcast(f32[768,32]{0,1:T(8,128)S(1)} %convert_bitcast_fusion), dimensions={0,1} | broadcast | bytes 6389760 | tf_op jit(solution)/shard_map/broadcast_in_dim | solution.py:11
  11.3 0.0 copy-start.1
  11.3 6.7 %copy.9 = f32[768,2048]{1,0:T(8,128)} copy(f32[768,2048]{0,1:T(8,128)} %bitcast.41) | data formatting | bytes 12582912 | tf_op jit(solution)/shard_map/convert_element_type | solution.py:11
  18.0 0.0 copy-done.1
  18.0 0.0 copy-start.2
  18.0 5.6 %multiply_convert_fusion = bf16[768,2048]{1,0:T(8,128)(2,1)} fusion(f32[768,2048]{1,0:T(8,128)} %copy.9, bf16[768,2048]{1,0:T(8,128)(2,1)S(1)} %copy-done.1, f32[2048]{0:T(1024)S(1)} %get-tuple-element.7, f32[2048]{0:T(1024)S(1)} %get-tuple-element.6), kind=kLoop, calls=%fused_computation.8 | loop fusion | flops 7864320 | bytes 12599296 | tf_op jit(solution)/shard_map/convert_element_type | solution.py:14
  23.6 0.0 all-gather.2.cloned.1.call-update
  23.7 0.0 reduce-scatter.2.cloned.1.call-start
  23.7 0.0 copy-done.2
  23.7 0.1 copy.8
  23.9 0.1 reduce
  24.0 0.7 fusion.17
  24.7 9.9 %compare_and_fusion.1 = pred[3072]{0:T(1024)(128)(4,1)S(1)} fusion(s32[]{:T(128)} %bitcast.32, s32[]{:T(128)} %bitcast.31, s32[]{:T(128)} %bitcast.30, s32[]{:T(128)} %bitcast.29, s32[]{:T(128)} %bitcast.28, s32[]{:T(128)} %bitcast.27, s32[]{:T(128)} %bitcast.26, s32[]{:T(128)} %bitcast.25, s32[]{:T(128)} %bitcast.24, s32[]{:T(128)} %bitcast.23, ...), kind=kLoop, calls=%fused_computation.25 | loop fusion | flops 168960 | bytes 3136 | tf_op jit(solution)/shard_map/jit(_take)/and | solution.py:25
  34.6 0.7 fusion.16
  35.3 10.2 %select_compare_fusion = pred[3072]{0:T(1024)(128)(4,1)S(1)} fusion(s32[]{:T(128)} %bitcast.15, s32[]{:T(128)} %bitcast.14, s32[]{:T(128)} %bitcast.13, s32[]{:T(128)} %bitcast.12, s32[]{:T(128)} %bitcast.11, s32[]{:T(128)} %bitcast.10, s32[]{:T(128)} %bitcast.9, s32[]{:T(128)} %bitcast.8, s32[]{:T(128)} %bitcast.7, s32[]{:T(128)} %bitcast.6, s32[]{:T(128)} %bitcast.5, ...), kind=kLoop, calls=%fused_computation.22 | loop fusion | flops 147456 | bytes 3136 | tf_op jit(solution)/shard_map/lt | solution.py:24
  45.5 9.9 %broadcast_clamp_fusion = s32[3072]{0:T(1024)S(1)} fusion(s32[]{:T(128)} %bitcast.32, s32[]{:T(128)} %bitcast.31, s32[]{:T(128)} %bitcast.30, s32[]{:T(128)} %bitcast.29, s32[]{:T(128)} %bitcast.28, s32[]{:T(128)} %bitcast.27, s32[]{:T(128)} %bitcast.26, s32[]{:T(128)} %bitcast.25, s32[]{:T(128)} %bitcast.24, s32[]{:T(128)} %bitcast.23, s32[]{:T(128)} %bitcast.22, ...), kind=kLoop, calls=%fused_computation.27 | loop fusion | flops 162816 | bytes 12352 | tf_op jit(solution)/shard_map/jit(_take)/gather | solution.py:25
  55.4 0.0 copy-start
  55.4 0.0 all-gather.2.cloned.1.call-done
  55.5 27.6 %gather_fusion = bf16[3072,2048]{1,0:T(8,128)(2,1)} fusion(bf16[1536,2048]{1,0:T(8,128)(2,1)} %all-gather.2.cloned.1.call-done, s32[3072]{0:T(1024)S(1)} %broadcast_clamp_fusion), kind=kCustom, calls=%fused_computation | custom fusion | bytes 25178112 | tf_op jit(solution)/shard_map/jit(_take)/gather | solution.py:25
  83.0 0.0 copy-done
  83.0 16.2 %fusion.7 = f32[3072,768]{1,0:T(8,128)} fusion(bf16[768,2048]{1,0:T(8,128)(2,1)S(1)} %copy-done, bf16[3072,2048]{1,0:T(8,128)(2,1)} %gather_fusion, pred[3072]{0:T(1024)(128)(4,1)S(1)} %compare_and_fusion.1, pred[3072]{0:T(1024)(128)(4,1)S(1)} %select_compare_fusion), kind=kOutput, calls=%fused_computation.9 | convolution fusion | flops 9678618624 | bytes 25171968 | tf_op jit(solution)/shard_map/rm,sm->rs/dot_general | solution.py:27
  99.2 0.0 reduce-scatter.2.cloned.1.call-update
  99.2 166.3 %reduce-scatter.2.cloned.1.call-done = f32[384,768]{1,0:T(8,128)} async-done(((f32[3072,768]{1,0:T(8,128)}), f32[384,768]{1,0:T(8,128)}) %reduce-scatter.2.cloned.1.call-update) | async-done | bytes 1179664 | tf_op jit(solution)/shard_map/reduce_scatter | solution.py:28
  265.5 5.8 %all_to_all.19 = f32[2,192,768]{2,1,0:T(8,128)S(1)} all-to-all(f32[2,192,768]{2,1,0:T(8,128)} %bitcast.43), channel_id=1, replica_groups=mesh['grp'=2,'mk'=8,'tile'=2] {'tile'}, dimensions={0} | all-to-all | bytes 2359296 | tf_op jit(solution)/shard_map/all_to_all | solution.py:31
  271.3 1.2 copy.11
  (2 shorter events, 0.0 us)
Async XLA Ops:
  6.5 48.9 %all-gather.2.cloned.1.call-start = ((), (), s32[]{:S(2)}) async-start(), calls=%async_computation.2 | async-start | bytes 9437184 | tf_op jit(solution)/shard_map/all_gather | solution.py:15
  11.3 6.7 %copy-start.1 = (bf16[768,2048]{1,0:T(8,128)(2,1)S(1)}, bf16[768,2048]{1,0:T(8,128)(2,1)}, u32[]{:S(2)}) copy-start(bf16[768,2048]{1,0:T(8,128)(2,1)} %param.6) | copy-start | bytes 9437188
  18.0 5.7 %copy-start.2 = (s32[16]{0:T(128)S(1)}, s32[16]{0:T(128)}, u32[]{:S(2)}) copy-start(s32[16]{0:T(128)} %param.9) | copy-start | bytes 196
  23.7 241.8 %reduce-scatter.2.cloned.1.call-start = ((), (), s32[]{:S(2)}) async-start(), calls=%async_computation.3 | async-start | bytes 10616832 | tf_op jit(solution)/shard_map/reduce_scatter | solution.py:28
  55.4 27.6 %copy-start = (bf16[768,2048]{1,0:T(8,128)(2,1)S(1)}, bf16[768,2048]{1,0:T(8,128)(2,1)}, u32[]{:S(2)}) copy-start(bf16[768,2048]{1,0:T(8,128)(2,1)} %multiply_convert_fusion) | copy-start | bytes 9437188
Sparse Core Ops, SparseCore 0:
  23.8 19.4 all-gather.1
  99.3 166.0 reduce-scatter.1
where the time goes:
time: 280 us; the launch traced here: 279 us
  waiting for transfers between devices  166 us (59%)
  local copies, waits for them, and re-layouts  40.1 us (14%)
  other arithmetic  37.4 us (13%)
  matrix products  16.2 us (6%)
  between operations  13.5 us (5%)
  blocking collectives  5.8 us (2%)
    reduce_scatter x1, waiting for transfers between devices, local(): lax.psum_scatter(product * (1.0 / marker_total), 'mk', scatter_dimension=...  166 us
    gather x1, local copies, waits for them, and re-layouts, local(): picked = jnp.take(all_rows, jnp.clip(sample_ids, 0, samples - 1), axis=0)  27.6 us
    dot_general x1, matrix products, local(): jnp.einsum('rm,sm->rs', picked, standard, preferred_element_type=jnp.floa...  16.2 us
    lt x1, other arithmetic, local(): live = within < jnp.take(panel_rows, owner_ids)  10.2 us
    and x1, other arithmetic, local(): picked = jnp.take(all_rows, jnp.clip(sample_ids, 0, samples - 1), axis=0)  9.9 us
    gather x1, other arithmetic, local(): picked = jnp.take(all_rows, jnp.clip(sample_ids, 0, samples - 1), axis=0)  9.88 us
    convert_element_type x1, local copies, waits for them, and re-layouts, local(): jnp.repeat(present.T, local_markers // present.shape[0], axis=1)  6.71 us
    all_to_all x1, blocking collectives, local(): lax.all_to_all(pair_rows, 'tile', split_axis=0, concat_axis=1, tiled=True)  5.8 us
  transfers between devices with their start and end apart: 2, of which 1 were waited for; matrix products, arithmetic and copies ran while one was open for 11% of the time, Pallas kernels for 0%

commit v1 on v0

--- a/solution.py
+++ b/solution.py
@@ -2,6 +2,13 @@
 import jax.numpy as jnp
 from jax import lax
 from jax.sharding import PartitionSpec as P
+
+
+def mark_screen(payload, axis_id):
+    reached = jnp.stack(jnp.split(payload, jax.lax.axis_size(axis_id), axis=0), axis=0)
+    met_up = jax.lax.all_to_all(reached, axis_name=axis_id, split_axis=0, concat_axis=0)
+    last = jnp.concatenate(met_up, axis=1)
+    return last
 
 
 def local(dosage, allele_freq, present, panel_rows):
@@ -28,7 +35,7 @@
     pair_rows = lax.psum_scatter(
         product * (1.0 / marker_total), "mk", scatter_dimension=0, tiled=True
     )
-    return lax.all_to_all(pair_rows, "tile", split_axis=0, concat_axis=1, tiled=True)
+    return mark_screen(pair_rows, "tile")
 
 
 def solution(mesh):

time: 280 us -> 280 us (level)
  no operation moved by 1% of the time
where the time goes in v1:
time: 280 us
  waiting for transfers between devices  166 us (59%)
  local copies, waits for them, and re-layouts  41.5 us (15%)
  other arithmetic  37.6 us (13%)
  matrix products  16.1 us (6%)
  between operations  13.5 us (5%)
  blocking collectives  4.68 us (2%)
    reduce_scatter x1, waiting for transfers between devices, local(): lax.psum_scatter(product * (1.0 / marker_total), 'mk', scatter_dimension=...  166 us
    gather x1, local copies, waits for them, and re-layouts, local(): picked = jnp.take(all_rows, jnp.clip(sample_ids, 0, samples - 1), axis=0)  27.6 us
    dot_general x1, matrix products, local(): jnp.einsum('rm,sm->rs', picked, standard, preferred_element_type=jnp.floa...  16.1 us
    lt x1, other arithmetic, local(): live = within < jnp.take(panel_rows, owner_ids)  10.1 us
    and x1, other arithmetic, local(): picked = jnp.take(all_rows, jnp.clip(sample_ids, 0, samples - 1), axis=0)  9.97 us
    gather x1, other arithmetic, local(): picked = jnp.take(all_rows, jnp.clip(sample_ids, 0, samples - 1), axis=0)  9.96 us
    convert_element_type x1, local copies, waits for them, and re-layouts, local(): jnp.repeat(present.T, local_markers // present.shape[0], axis=1)  6.78 us
    convert_element_type x1, other arithmetic, local(): standard = (flags * scaled).astype(jnp.bfloat16)  5.63 us
  transfers between devices with their start and end apart: 2, of which 1 were waited for; matrix products, arithmetic and copies ran while one was open for 11% of the time, Pallas kernels for 0%

profile of v1, /device:TPU:0, one launch (start us, length us, event | category | flops | bytes accessed | tf_op | source)
XLA Modules:
  0.0 279.8 jit_solution(1414188013923625936)
XLA Ops:
  6.5 0.0 all-gather.2.cloned.1.call-start
  6.5 0.7 broadcast_multiply_fusion
  7.2 0.9 convert_bitcast_fusion
  8.1 3.1 %broadcast_in_dim.38 = f32[768,32,64]{0,2,1:T(8,128)} broadcast(f32[768,32]{0,1:T(8,128)S(1)} %convert_bitcast_fusion), dimensions={0,1} | broadcast | bytes 6389760 | tf_op jit(solution)/shard_map/broadcast_in_dim | solution.py:18
  11.3 0.0 copy-start.1
  11.3 6.8 %copy.8 = f32[768,2048]{1,0:T(8,128)} copy(f32[768,2048]{0,1:T(8,128)} %bitcast.44) | data formatting | bytes 12582912 | tf_op jit(solution)/shard_map/convert_element_type | solution.py:18
  18.1 0.0 copy-done.1
  18.1 0.0 copy-start.2
  18.1 5.6 %multiply_convert_fusion = bf16[768,2048]{1,0:T(8,128)(2,1)} fusion(f32[768,2048]{1,0:T(8,128)} %copy.8, bf16[768,2048]{1,0:T(8,128)(2,1)S(1)} %copy-done.1, f32[2048]{0:T(1024)S(1)} %get-tuple-element.9, f32[2048]{0:T(1024)S(1)} %get-tuple-element.8), kind=kLoop, calls=%fused_computation.8 | loop fusion | flops 7864320 | bytes 12599296 | tf_op jit(solution)/shard_map/convert_element_type | solution.py:21
  23.7 0.0 all-gather.2.cloned.1.call-update
  23.7 0.0 reduce-scatter.2.cloned.1.call-start
  23.8 0.0 copy-done.2
  23.8 0.1 copy.7
  23.9 0.1 reduce
  24.0 0.7 fusion.17
  24.7 10.0 %compare_and_fusion.1 = pred[3072]{0:T(1024)(128)(4,1)S(1)} fusion(s32[]{:T(128)} %bitcast.32, s32[]{:T(128)} %bitcast.31, s32[]{:T(128)} %bitcast.30, s32[]{:T(128)} %bitcast.29, s32[]{:T(128)} %bitcast.28, s32[]{:T(128)} %bitcast.27, s32[]{:T(128)} %bitcast.26, s32[]{:T(128)} %bitcast.25, s32[]{:T(128)} %bitcast.24, s32[]{:T(128)} %bitcast.23, ...), kind=kLoop, calls=%fused_computation.28 | loop fusion | flops 168960 | bytes 3136 | tf_op jit(solution)/shard_map/jit(_take)/and | solution.py:32
  34.7 0.7 fusion.16
  35.4 10.1 %select_compare_fusion = pred[3072]{0:T(1024)(128)(4,1)S(1)} fusion(s32[]{:T(128)} %bitcast.15, s32[]{:T(128)} %bitcast.14, s32[]{:T(128)} %bitcast.13, s32[]{:T(128)} %bitcast.12, s32[]{:T(128)} %bitcast.11, s32[]{:T(128)} %bitcast.10, s32[]{:T(128)} %bitcast.9, s32[]{:T(128)} %bitcast.8, s32[]{:T(128)} %bitcast.7, s32[]{:T(128)} %bitcast.6, s32[]{:T(128)} %bitcast.5, ...), kind=kLoop, calls=%fused_computation.25 | loop fusion | flops 147456 | bytes 3136 | tf_op jit(solution)/shard_map/lt | solution.py:31
  45.6 10.0 %broadcast_clamp_fusion = s32[3072]{0:T(1024)S(1)} fusion(s32[]{:T(128)} %bitcast.32, s32[]{:T(128)} %bitcast.31, s32[]{:T(128)} %bitcast.30, s32[]{:T(128)} %bitcast.29, s32[]{:T(128)} %bitcast.28, s32[]{:T(128)} %bitcast.27, s32[]{:T(128)} %bitcast.26, s32[]{:T(128)} %bitcast.25, s32[]{:T(128)} %bitcast.24, s32[]{:T(128)} %bitcast.23, s32[]{:T(128)} %bitcast.22, ...), kind=kLoop, calls=%fused_computation.30 | loop fusion | flops 162816 | bytes 12352 | tf_op jit(solution)/shard_map/jit(_take)/gather | solution.py:32
  55.6 0.0 copy-start
  55.6 0.0 all-gather.2.cloned.1.call-done
  55.6 27.6 %gather_fusion = bf16[3072,2048]{1,0:T(8,128)(2,1)} fusion(bf16[1536,2048]{1,0:T(8,128)(2,1)} %all-gather.2.cloned.1.call-done, s32[3072]{0:T(1024)S(1)} %broadcast_clamp_fusion), kind=kCustom, calls=%fused_computation | custom fusion | bytes 25178112 | tf_op jit(solution)/shard_map/jit(_take)/gather | solution.py:32
  83.2 0.0 copy-done
  83.2 16.1 %fusion.7 = f32[3072,768]{1,0:T(8,128)} fusion(bf16[768,2048]{1,0:T(8,128)(2,1)S(1)} %copy-done, bf16[3072,2048]{1,0:T(8,128)(2,1)} %gather_fusion, pred[3072]{0:T(1024)(128)(4,1)S(1)} %compare_and_fusion.1, pred[3072]{0:T(1024)(128)(4,1)S(1)} %select_compare_fusion), kind=kOutput, calls=%fused_computation.9 | convolution fusion | flops 9678618624 | bytes 25171968 | tf_op jit(solution)/shard_map/rm,sm->rs/dot_general | solution.py:34
  99.3 0.0 reduce-scatter.2.cloned.1.call-update
  99.3 166.3 %reduce-scatter.2.cloned.1.call-done = f32[384,768]{1,0:T(8,128)} async-done(((f32[3072,768]{1,0:T(8,128)}), f32[384,768]{1,0:T(8,128)}) %reduce-scatter.2.cloned.1.call-update) | async-done | bytes 1179664 | tf_op jit(solution)/shard_map/reduce_scatter | solution.py:35
  265.7 1.3 slice_bitcast_fusion.1
  267.0 0.1 pad_maximum_fusion
  267.1 4.7 %all_to_all.5 = f32[2,192,768]{2,1,0:T(8,128)S(1)} all-to-all(f32[2,192,768]{2,1,0:T(8,128)S(1)} %pad_maximum_fusion), channel_id=1, replica_groups=mesh['grp'=2,'mk'=8,'tile'=2] {'tile'}, dimensions={0} | all-to-all | bytes 2359296 | tf_op jit(solution)/shard_map/all_to_all | solution.py:9
  271.8 1.2 copy.10
  (2 shorter events, 0.0 us)
Async XLA Ops:
  6.5 49.1 %all-gather.2.cloned.1.call-start = ((), (), s32[]{:S(2)}) async-start(), calls=%async_computation.2 | async-start | bytes 9437184 | tf_op jit(solution)/shard_map/all_gather | solution.py:22
  11.3 6.8 %copy-start.1 = (bf16[768,2048]{1,0:T(8,128)(2,1)S(1)}, bf16[768,2048]{1,0:T(8,128)(2,1)}, u32[]{:S(2)}) copy-start(bf16[768,2048]{1,0:T(8,128)(2,1)} %param.6) | copy-start | bytes 9437188
  18.1 5.7 %copy-start.2 = (s32[16]{0:T(128)S(1)}, s32[16]{0:T(128)}, u32[]{:S(2)}) copy-start(s32[16]{0:T(128)} %param.9) | copy-start | bytes 196
  23.7 241.9 %reduce-scatter.2.cloned.1.call-start = ((), (), s32[]{:S(2)}) async-start(), calls=%async_computation.3 | async-start | bytes 10616832 | tf_op jit(solution)/shard_map/reduce_scatter | solution.py:35
  55.6 27.6 %copy-start = (bf16[768,2048]{1,0:T(8,128)(2,1)S(1)}, bf16[768,2048]{1,0:T(8,128)(2,1)}, u32[]{:S(2)}) copy-start(bf16[768,2048]{1,0:T(8,128)(2,1)} %multiply_convert_fusion) | copy-start | bytes 9437188
Sparse Core Ops, SparseCore 0:
  23.9 19.4 all-gather.1
  99.5 166.1 reduce-scatter.1
